TPU v7x, 32 devices: a whole 2x2x4 slice. The times are simulated.
32 devices in a mesh: axial: 8 (over z, x), cross: 4 (over y, core).
Axes of the slice: x: 2, y: 2, z: 4, core: 2. Of those that a mesh axis runs over, the one named last changes fastest.
Arguments:
- cotangent: float32 [128, 32, 16, 128], P('axial', None, 'cross'), may hold values from -8 to 8
- diag_blocks: float32 [128, 32, 32], P('axial'), as said below
- lower_rates: float32 [128, 32], P('axial'), as said below
- upper_rates: float32 [128, 32], P('axial'), as said below
- cross_rate: float32 [32], replicated, may hold values from 0.02 to 0.24
- bin_profile: float32 [32], replicated, may hold values from 0.1 to 1
- open_cells: int32 [16, 128], replicated, may hold values 0 or 1
- segment_ids: int32 [128, 16], P('axial', 'cross'), may hold values from 0 to 127
Outputs:
- grad_state: float32 [128, 32, 16, 128], P('axial', None, 'cross')
- grad_emission: float32 [128], P(('axial', 'cross'))
Inputs may be any that keep to these rules, and one draw needn't show every extreme that they name: In every row (i, b) of the forward operator, diag_blocks[i, b, b] exceeds lower_rates[i, b] + upper_rates[i, b] + the sum of the magnitudes of the other entries of diag_blocks[i, b, :] by 1 or more. `lower_rates`: Positive. `upper_rates`: Positive.
All inputs are finite; a program needn't handle non-finite values.
Results may differ from a plain program's by a relative error of at most 0.0003.
Values sent between devices are 32-bit elements; how exact they have to be, the bound alone decides.
A program may use at most 64 MiB of HBM per device.

v0:
```python
import jax
import jax.numpy as jnp
from jax import lax
from jax.sharding import PartitionSpec as P

SEG_DEV = 4


exact_precision = lax.Precision.HIGHEST


def passed_along(value, axis, steps):
    count = lax.axis_size(axis)
    first, last = (max(0, -steps), min(count, count - steps))
    return lax.ppermute(value, axis, [(source, source + steps) for source in range(first, last)])


def with_halo(cells, sides, width):
    for axis, dim in sides:
        count = lax.axis_size(axis)
        ends = count - 1
        head = lax.slice_in_dim(cells, 0, width, axis=dim)
        tail = lax.slice_in_dim(cells, cells.shape[dim] - width, cells.shape[dim], axis=dim)
        cells = jnp.concatenate(
            [
                lax.ppermute(tail, axis, [(i, (i + 1) % count) for i in range(ends)]),
                cells,
                lax.ppermute(head, axis, [((i + 1) % count, i) for i in range(ends)]),
            ],
            axis=dim,
        )
    return cells


def product(left_mat, right_mat):
    return jnp.matmul(left_mat, right_mat, precision=exact_precision)


def invert(matrices):
    dimension = matrices.shape[-1]
    identity = jnp.eye(dimension, dtype=matrices.dtype)
    diag_values = jnp.diagonal(matrices, axis1=-2, axis2=-1)
    estimate = identity * (1.0 / diag_values)[..., None, :]
    for sweep in range(10):
        residual_term = 2.0 * identity - product(matrices, estimate)
        estimate = product(estimate, residual_term)
    return estimate


def select_row(payload, index):
    return tuple((member[index : index + 1] for member in payload))


def join_rows(upper_part, lower_part):
    return tuple(
        (
            jnp.concatenate([first_member, second_member], axis=0)
            for first_member, second_member in zip(upper_part, lower_part)
        )
    )


def from_left(payload, stride):
    return passed_along(payload, "axial", stride)


def from_right(payload, stride):
    return passed_along(payload, "axial", -stride)


def eliminate(current, centre_block, left_side, right_side):
    lower_block, upper_block, inverse, source = current
    left_lower, left_upper, left_inverse, left_source = left_side
    right_lower, right_upper, right_inverse, right_source = right_side
    left_factor = -product(lower_block, left_inverse)
    right_factor = -product(upper_block, right_inverse)
    centre_block = (
        centre_block + product(left_factor, left_upper) + product(right_factor, right_lower)
    )
    source = source + product(left_factor, left_source) + product(right_factor, right_source)
    updated = (
        product(left_factor, left_lower),
        product(right_factor, right_upper),
        invert(centre_block),
        source,
    )
    return (updated, centre_block)


def per_device(
    cotangent,
    diag_blocks,
    lower_rates,
    upper_rates,
    cross_rate,
    bin_profile,
    open_cells,
    segment_ids,
):
    cell_count, bin_count, rows_dev, depth_cells = cotangent.shape
    line_count = rows_dev * depth_cells
    last_cell = cell_count - 1
    n_int = cell_count - 2
    source_all = cotangent.reshape(cell_count, bin_count, line_count)
    rims = with_halo(jnp.stack([upper_rates, lower_rates]), (("axial", 1),), 1)
    below_rate = -rims[0, :cell_count]
    above_rate = -rims[1, 2:]
    adjoint_diag = jnp.swapaxes(diag_blocks, 1, 2)
    identity = jnp.eye(bin_count, dtype=jnp.float32)
    spike_source = jnp.zeros((n_int, bin_count, 2 * bin_count), jnp.float32)
    spike_source = spike_source.at[0, :, :bin_count].set(-below_rate[1][:, None] * identity)
    spike_source = spike_source.at[n_int - 1, :, bin_count:].set(
        -above_rate[last_cell - 1][:, None] * identity
    )

    def forward(state_carry, inputs):
        inverse_prev, field_prev, spike_prev = state_carry
        a_vec, c_last, diag_block, field_source, spike_in = inputs
        weight = a_vec[:, None] * inverse_prev
        inverse_now = invert(diag_block - weight * c_last[None, :])
        field_now = field_source - product(weight, field_prev)
        spike_now = spike_in - product(weight, spike_prev)
        return ((inverse_now, field_now, spike_now), (inverse_now, field_now, spike_now))

    start_state = (
        jnp.zeros((bin_count, bin_count), jnp.float32),
        jnp.zeros((bin_count, line_count), jnp.float32),
        jnp.zeros((bin_count, 2 * bin_count), jnp.float32),
    )
    inputs_forward = (
        below_rate[1:last_cell],
        above_rate[0 : last_cell - 1],
        adjoint_diag[1:last_cell],
        source_all[1:last_cell],
        spike_source,
    )
    _, (inverses, fields, spikes) = lax.scan(forward, start_state, inputs_forward)

    def backward(state_carry, inputs):
        field_next, spike_next = state_carry
        inverse_now, field_now, spike_now, c_vec = inputs
        field_next = product(inverse_now, field_now - c_vec[:, None] * field_next)
        spike_next = product(inverse_now, spike_now - c_vec[:, None] * spike_next)
        return ((field_next, spike_next), (field_next, spike_next))

    end_state = (
        jnp.zeros((bin_count, line_count), jnp.float32),
        jnp.zeros((bin_count, 2 * bin_count), jnp.float32),
    )
    _, (inner_field, inner_spike) = lax.scan(
        backward, end_state, (inverses, fields, spikes, above_rate[1:last_cell]), reverse=True
    )
    first_spike = inner_spike[0]
    end_spike = inner_spike[n_int - 1]
    head_scale = above_rate[0][:, None]
    tail_scale = below_rate[last_cell][:, None]
    lower_block = jnp.stack(
        [identity * below_rate[0][:, None], tail_scale * end_spike[:, :bin_count]]
    )
    upper_block = jnp.stack(
        [head_scale * first_spike[:, bin_count:], identity * above_rate[last_cell][:, None]]
    )
    centre_block = jnp.stack(
        [
            adjoint_diag[0] + head_scale * first_spike[:, :bin_count],
            adjoint_diag[last_cell] + tail_scale * end_spike[:, bin_count:],
        ]
    )
    source = jnp.stack(
        [
            source_all[0] - head_scale * inner_field[0],
            source_all[last_cell] - tail_scale * inner_field[n_int - 1],
        ]
    )
    current = (lower_block, upper_block, invert(centre_block), source)
    far_right = from_right(select_row(current, 0), 1)
    far_left = from_left(select_row(current, 1), 1)
    current, centre_block = eliminate(
        current,
        centre_block,
        join_rows(far_left, select_row(current, 0)),
        join_rows(select_row(current, 1), far_right),
    )
    axial_count = lax.axis_size("axial")
    stride = 1
    while stride < axial_count:
        current, centre_block = eliminate(
            current, centre_block, from_left(current, stride), from_right(current, stride)
        )
        stride = stride * 2
    solved = product(current[2], current[3])
    start_value = solved[0]
    end_value = solved[1]
    both_ends = jnp.concatenate([start_value, end_value], axis=0)
    interior = inner_field + product(inner_spike, both_ends)
    adjoint = jnp.concatenate([start_value[None], interior, end_value[None]], axis=0)
    adjoint = adjoint.reshape(cell_count, bin_count, rows_dev, depth_cells)
    padded = with_halo(adjoint, (("cross", 2),), 1)
    padded = jnp.pad(padded, ((0, 0), (0, 0), (0, 0), (1, 1)))
    mask_all = jnp.pad(open_cells.astype(jnp.float32), 1)
    mask_local = lax.dynamic_slice_in_dim(
        mask_all, lax.axis_index("cross") * rows_dev, rows_dev + 2, 0
    )
    centre_mask = mask_local[1:-1, 1:-1]
    flux_sum = jnp.zeros_like(adjoint)
    for shift_y, shift_z in ((0, 1), (2, 1), (1, 0), (1, 2)):
        neighbour_mask = mask_local[shift_y : shift_y + rows_dev, shift_z : shift_z + depth_cells]
        neighbour = padded[:, :, shift_y : shift_y + rows_dev, shift_z : shift_z + depth_cells]
        flux_sum = flux_sum + neighbour_mask * (neighbour - adjoint)
    grad_state = adjoint + cross_rate[None, :, None, None] * centre_mask * flux_sum
    emitted = jnp.einsum("ibyz,yz->iby", adjoint, centre_mask, precision=exact_precision)
    emitted = jnp.einsum("iby,b->iy", emitted, bin_profile, precision=exact_precision) / depth_cells
    emitted_flat = emitted.reshape(-1)
    segment_flat = segment_ids.reshape(-1)
    wanted = lax.iota(jnp.int32, SEG_DEV * lax.axis_size(("axial", "cross")))
    onehot = (segment_flat[:, None] == wanted[None, :]).astype(jnp.float32)
    grad_emission = lax.psum_scatter(
        jnp.dot(emitted_flat, onehot, precision=exact_precision),
        ("axial", "cross"),
        scatter_dimension=0,
        tiled=True,
    )
    return (grad_state, grad_emission)


def solution(mesh):
    in_specs = (
        P("axial", None, "cross", None),
        P("axial", None, None),
        P("axial", None),
        P("axial", None),
        P(),
        P(),
        P(),
        P("axial", "cross"),
    )
    out_specs = (P("axial", None, "cross", None), P(("axial", "cross")))
    return jax.shard_map(
        per_device, mesh=mesh, in_specs=in_specs, out_specs=out_specs, check_vma=False
    )
```

profile of v0, /device:TPU:0, one launch (start us, length us, event | category | flops | bytes accessed | tf_op | source)
XLA Modules:
  0.0 344.7 jit_solution(5758030535908721834)
XLA Ops:
  1.4 4.8 %collective-permute-start.1 = (f32[2,1,32]{2,1,0:T(1,128)S(1)}, f32[2,1,32]{2,1,0:T(1,128)S(1)}, u32[]{:S(2)}, u32[]{:S(2)}) collective-permute-start(f32[2,1,32]{2,1,0:T(1,128)S(1)} %get-tuple-element.399), channel_id=1, source_target_pairs={{0,4},{4,8},{8,12},{12,16},{16,20},{20,24},{24,28},{1,5},{5,9},{9,... | collective-permute-start | bytes 776 | tf_op jit(solution)/shard_map/ppermute | solution.py:26
  16.8 5.1 %collective-permute-start.3 = (f32[1,32,32]{2,1,0:T(8,128)S(1)}, f32[1,32,32]{2,1,0:T(8,128)}, u32[]{:S(2)}, u32[]{:S(2)}) collective-permute-start(f32[1,32,32]{2,1,0:T(8,128)S(1)} %fusion.129), channel_id=1, source_target_pairs={{0,4},{4,8},{8,12},{12,16},{16,20},{20,24},{24,28},{1,5},{5,9},{9,... | collective-permute-start | bytes 12296 | tf_op jit(solution)/shard_map/ppermute | solution.py:15
  24.5 69.9 %while.44 = (s32[]{:T(128)}, f32[32,32]{1,0:T(8,128)S(1)}, f32[32,512]{1,0:T(8,128)S(1)}, f32[32,64]{1,0:T(8,128)S(1)}, f32[14,32,32]{2,1,0:T(8,128)}, /*index=5...) while((s32[]{:T(128)}, f32[32,32]{1,0:T(8,128)S(1)}, ...), condition=%wide.region_1.0_spmd.clone, body=%wide.region_0.0_spmd.clone.sunk | while | flops 15019171 | bytes 777260 | solution.py:137
  94.6 37.0 %while.43 = (s32[]{:T(128)}, f32[32,512]{1,0:T(8,128)S(1)}, f32[32,64]{1,0:T(8,128)S(1)}, f32[14,32,512]{2,1,0:T(8,128)S(1)}, f32[14,32,64]{2,1,0:T(8,128)S(1)},...) while((s32[]{:T(128)}, f32[32,512]{1,0:T(8,128)S(1)}, ...), condition=%wide.region_3.4_spmd, body=%wide.region_2.3_spmd.sunk | while | flops 7114755 | bytes 512381 | solution.py:150
  132.4 4.5 %collective-permute-start.6 = (f32[1,32,32]{2,1,0:T(8,128)S(1)}, f32[1,32,32]{2,1,0:T(8,128)S(1)}, u32[]{:S(2)}, u32[]{:S(2)}) collective-permute-start(f32[1,32,32]{2,1,0:T(8,128)S(1)} %get-tuple-element.392), channel_id=1, source_target_pairs={{0,4},{4,8},{8,12},{12,16},{16,20},{20,24},{24,28},{1,5},{5,9},{9,... | collective-permute-start | bytes 12296 | tf_op jit(solution)/shard_map/ppermute | solution.py:15
  144.2 5.6 %collective-permute-done.4 = f32[1,32,32]{2,1,0:T(8,128)S(1)} collective-permute-done((f32[1,32,32]{2,1,0:T(8,128)S(1)}, f32[1,32,32]{2,1,0:T(8,128)S(1)}, u32[]{:S(2)}, u32[]{:S(2)}) %collective-permute-start.4) | collective-permute-done | bytes 4128 | tf_op jit(solution)/shard_map/ppermute | solution.py:15
  149.8 4.8 %collective-permute-start.2 = (f32[1,32,32]{2,1,0:T(8,128)S(1)}, f32[1,32,32]{2,1,0:T(8,128)S(1)}, u32[]{:S(2)}, u32[]{:S(2)}) collective-permute-start(f32[1,32,32]{2,1,0:T(8,128)S(1)} %get-tuple-element.384), channel_id=1, source_target_pairs={{0,4},{4,8},{8,12},{12,16},{16,20},{20,24},{24,28},{1,5},{5,9},{9,... | collective-permute-start | bytes 12296 | tf_op jit(solution)/shard_map/ppermute | solution.py:15
  156.3 4.6 %collective-permute-start.24 = (f32[1,32,512]{2,1,0:T(8,128)S(1)}, f32[1,32,512]{2,1,0:T(8,128)S(1)}, u32[]{:S(2)}, u32[]{:S(2)}) collective-permute-start(f32[1,32,512]{2,1,0:T(8,128)S(1)} %get-tuple-element.374), channel_id=1, source_target_pairs={{0,4},{4,8},{8,12},{12,16},{16,20},{20,24},{24,28},{1,5},{5,9},{9,... | collective-permute-start | bytes 196616 | tf_op jit(solution)/shard_map/ppermute | solution.py:15
  163.2 5.4 %collective-permute-start.9 = (f32[2,32,32]{2,1,0:T(8,128)S(1)}, f32[2,32,32]{2,1,0:T(8,128)S(1)}, u32[]{:S(2)}, u32[]{:S(2)}) collective-permute-start(f32[2,32,32]{2,1,0:T(8,128)S(1)} %fusion.108), channel_id=1, source_target_pairs={{0,4},{4,8},{8,12},{12,16},{16,20},{20,24},{24,28},{1,5},{5,9},{9,... | collective-permute-start | bytes 24584 | tf_op jit(solution)/shard_map/ppermute | solution.py:15
  175.5 5.2 %collective-permute-done.10 = f32[2,32,32]{2,1,0:T(8,128)S(1)} collective-permute-done((f32[2,32,32]{2,1,0:T(8,128)S(1)}, f32[2,32,32]{2,1,0:T(8,128)S(1)}, u32[]{:S(2)}, u32[]{:S(2)}) %collective-permute-start.10) | collective-permute-done | bytes 8224 | tf_op jit(solution)/shard_map/ppermute | solution.py:15
  180.7 4.8 %collective-permute-start.12 = (f32[2,32,32]{2,1,0:T(8,128)S(1)}, f32[2,32,32]{2,1,0:T(8,128)S(1)}, u32[]{:S(2)}, u32[]{:S(2)}) collective-permute-start(f32[2,32,32]{2,1,0:T(8,128)S(1)} %fusion.104), channel_id=1, source_target_pairs={{0,4},{4,8},{8,12},{12,16},{16,20},{20,24},{24,28},{1,5},{5,9},{9,... | collective-permute-start | bytes 24584 | tf_op jit(solution)/shard_map/ppermute | solution.py:15
  187.2 4.3 %collective-permute-done.11 = f32[2,32,32]{2,1,0:T(8,128)S(1)} collective-permute-done((f32[2,32,32]{2,1,0:T(8,128)S(1)}, f32[2,32,32]{2,1,0:T(8,128)S(1)}, u32[]{:S(2)}, u32[]{:S(2)}) %collective-permute-start.11) | collective-permute-done | bytes 8224 | tf_op jit(solution)/shard_map/ppermute | solution.py:15
  197.5 6.3 %collective-permute-start.15 = (f32[2,32,32]{2,1,0:T(8,128)S(1)}, f32[2,32,32]{2,1,0:T(8,128)S(1)}, u32[]{:S(2)}, u32[]{:S(2)}) collective-permute-start(f32[2,32,32]{2,1,0:T(8,128)S(1)} %fusion.202), channel_id=1, source_target_pairs={{0,8},{4,12},{8,16},{12,20},{16,24},{20,28},{1,9},{5,13},{9,17},{1... | collective-permute-start | bytes 24584 | tf_op jit(solution)/shard_map/ppermute | solution.py:15
  209.9 4.6 %collective-permute-done.16 = f32[2,32,32]{2,1,0:T(8,128)S(1)} collective-permute-done((f32[2,32,32]{2,1,0:T(8,128)S(1)}, f32[2,32,32]{2,1,0:T(8,128)S(1)}, u32[]{:S(2)}, u32[]{:S(2)}) %collective-permute-start.16) | collective-permute-done | bytes 8224 | tf_op jit(solution)/shard_map/ppermute | solution.py:15
  214.5 3.6 %collective-permute-start.13 = (f32[2,32,32]{2,1,0:T(8,128)S(1)}, f32[2,32,32]{2,1,0:T(8,128)S(1)}, u32[]{:S(2)}, u32[]{:S(2)}) collective-permute-start(f32[2,32,32]{2,1,0:T(8,128)S(1)} %fusion.201), channel_id=1, source_target_pairs={{0,8},{4,12},{8,16},{12,20},{16,24},{20,28},{1,9},{5,13},{9,17},{1... | collective-permute-start | bytes 24584 | tf_op jit(solution)/shard_map/ppermute | solution.py:15
  221.2 4.6 %collective-permute-done.17 = f32[2,32,32]{2,1,0:T(8,128)S(1)} collective-permute-done((f32[2,32,32]{2,1,0:T(8,128)S(1)}, f32[2,32,32]{2,1,0:T(8,128)S(1)}, u32[]{:S(2)}, u32[]{:S(2)}) %collective-permute-start.17) | collective-permute-done | bytes 8224 | tf_op jit(solution)/shard_map/ppermute | solution.py:15
  225.9 3.9 %collective-permute-start.18 = (f32[2,32,32]{2,1,0:T(8,128)S(1)}, f32[2,32,32]{2,1,0:T(8,128)S(1)}, u32[]{:S(2)}, u32[]{:S(2)}) collective-permute-start(f32[2,32,32]{2,1,0:T(8,128)S(1)} %fusion.192), channel_id=1, source_target_pairs={{0,8},{4,12},{8,16},{12,20},{16,24},{20,28},{1,9},{5,13},{9,17},{1... | collective-permute-start | bytes 24584 | tf_op jit(solution)/shard_map/ppermute | solution.py:15
  235.9 5.4 %collective-permute-start.19 = (f32[2,32,32]{2,1,0:T(8,128)S(1)}, f32[2,32,32]{2,1,0:T(8,128)S(1)}, u32[]{:S(2)}, u32[]{:S(2)}) collective-permute-start(f32[2,32,32]{2,1,0:T(8,128)S(1)} %fusion.213), channel_id=1, source_target_pairs={{0,16},{4,20},{8,24},{12,28},{1,17},{5,21},{9,25},{13,29},{2,18},{... | collective-permute-start | bytes 24584 | tf_op jit(solution)/shard_map/ppermute | solution.py:15
  244.8 4.9 %collective-permute-done.23 = f32[2,32,32]{2,1,0:T(8,128)S(1)} collective-permute-done((f32[2,32,32]{2,1,0:T(8,128)S(1)}, f32[2,32,32]{2,1,0:T(8,128)S(1)}, u32[]{:S(2)}, u32[]{:S(2)}) %collective-permute-start.23) | collective-permute-done | bytes 8224 | tf_op jit(solution)/shard_map/ppermute | solution.py:15
  256.0 4.6 %collective-permute-start.26 = (f32[2,32,512]{2,1,0:T(8,128)S(1)}, f32[2,32,512]{2,1,0:T(8,128)S(1)}, u32[]{:S(2)}, u32[]{:S(2)}) collective-permute-start(f32[2,32,512]{2,1,0:T(8,128)S(1)} %fusion.39), channel_id=1, source_target_pairs={{0,4},{4,8},{8,12},{12,16},{16,20},{20,24},{24,28},{1,5},{5,9},{9,... | collective-permute-start | bytes 393224 | tf_op jit(solution)/shard_map/ppermute | solution.py:15
  264.8 5.7 %collective-permute-start.28 = (f32[2,32,512]{2,1,0:T(8,128)S(1)}, f32[2,32,512]{2,1,0:T(8,128)S(1)}, u32[]{:S(2)}, u32[]{:S(2)}) collective-permute-start(f32[2,32,512]{2,1,0:T(8,128)S(1)} %fusion.40), channel_id=1, source_target_pairs={{0,8},{4,12},{8,16},{12,20},{16,24},{20,28},{1,9},{5,13},{9,17},{1... | collective-permute-start | bytes 393224 | tf_op jit(solution)/shard_map/ppermute | solution.py:15
  274.8 5.8 %collective-permute-start.30 = (f32[2,32,512]{2,1,0:T(8,128)S(1)}, f32[2,32,512]{2,1,0:T(8,128)S(1)}, u32[]{:S(2)}, u32[]{:S(2)}) collective-permute-start(f32[2,32,512]{2,1,0:T(8,128)S(1)} %fusion.41), channel_id=1, source_target_pairs={{0,16},{4,20},{8,24},{12,28},{1,17},{5,21},{9,25},{13,29},{2,18},{... | collective-permute-start | bytes 393224 | tf_op jit(solution)/shard_map/ppermute | solution.py:15
  284.7 4.2 %fusion.47 = f32[4,1,16,32]{3,1,2,0:T(1,128)S(1)} fusion(f32[4,128,1,1]{1,2,3,0:T(1,128)S(1)} %bitcast.507, f32[16,4,4,8,128]{4,3,2,1,0:T(8,128)S(1)} %get-tuple-element.368), kind=kOutput, calls=%fused_computation.151 | convolution fusion | flops 3145728 | bytes 1058816 | tf_op jit(solution)/shard_map/ibyz,yz->iby/dot_general | solution.py:211
  293.2 44.5 %all-reduce.3 = f32[128]{0:T(128)S(1)} all-reduce(f32[128]{0:T(128)S(1)} %convolution_bitcast_fusion), channel_id=2, replica_groups=mesh['axial'=8,'cross'=4] {'axial','cross'}, use_global_device_ids=true, to_apply=%region_4.5.clone | all-reduce | flops 128 | bytes 1024
  (753 shorter events, 192.4 us)
Async XLA Ops:
  1.4 14.7 %collective-permute-start.1 = (f32[2,1,32]{2,1,0:T(1,128)S(1)}, f32[2,1,32]{2,1,0:T(1,128)S(1)}, u32[]{:S(2)}, u32[]{:S(2)}) collective-permute-start(f32[2,1,32]{2,1,0:T(1,128)S(1)} %get-tuple-element.399), channel_id=1, source_target_pairs={{0,4},{4,8},{8,12},{12,16},{16,20},{20,24},{24,28},{1,5},{5,9},{9,... | collective-permute-start | bytes 776 | tf_op jit(solution)/shard_map/ppermute | solution.py:26
  6.3 9.9 %collective-permute-start = (f32[2,1,32]{2,1,0:T(1,128)S(1)}, f32[2,1,32]{2,1,0:T(1,128)S(1)}, u32[]{:S(2)}, u32[]{:S(2)}) collective-permute-start(f32[2,1,32]{2,1,0:T(1,128)S(1)} %get-tuple-element.400), channel_id=1, source_target_pairs={{4,0},{8,4},{12,8},{16,12},{20,16},{24,20},{28,24},{5,1},{9,5},{13... | collective-permute-start | bytes 776 | tf_op jit(solution)/shard_map/ppermute | solution.py:28
  16.8 146.4 %collective-permute-start.3 = (f32[1,32,32]{2,1,0:T(8,128)S(1)}, f32[1,32,32]{2,1,0:T(8,128)}, u32[]{:S(2)}, u32[]{:S(2)}) collective-permute-start(f32[1,32,32]{2,1,0:T(8,128)S(1)} %fusion.129), channel_id=1, source_target_pairs={{0,4},{4,8},{8,12},{12,16},{16,20},{20,24},{24,28},{1,5},{5,9},{9,... | collective-permute-start | bytes 12296 | tf_op jit(solution)/shard_map/ppermute | solution.py:15
  22.0 134.3 %collective-permute-start.5 = (f32[1,32,32]{2,1,0:T(8,128)S(1)}, f32[1,32,32]{2,1,0:T(8,128)}, u32[]{:S(2)}, u32[]{:S(2)}) collective-permute-start(f32[1,32,32]{2,1,0:T(8,128)S(1)} %fusion.130), channel_id=1, source_target_pairs={{4,0},{8,4},{12,8},{16,12},{20,16},{24,20},{28,24},{5,1},{9,5},{13... | collective-permute-start | bytes 12296 | tf_op jit(solution)/shard_map/ppermute | solution.py:15
  132.4 41.6 %collective-permute-start.6 = (f32[1,32,32]{2,1,0:T(8,128)S(1)}, f32[1,32,32]{2,1,0:T(8,128)S(1)}, u32[]{:S(2)}, u32[]{:S(2)}) collective-permute-start(f32[1,32,32]{2,1,0:T(8,128)S(1)} %get-tuple-element.392), channel_id=1, source_target_pairs={{0,4},{4,8},{8,12},{12,16},{16,20},{20,24},{24,28},{1,5},{5,9},{9,... | collective-permute-start | bytes 12296 | tf_op jit(solution)/shard_map/ppermute | solution.py:15
  136.9 17.8 %collective-permute-start.8 = (f32[1,32,32]{2,1,0:T(8,128)S(1)}, f32[1,32,32]{2,1,0:T(8,128)S(1)}, u32[]{:S(2)}, u32[]{:S(2)}) collective-permute-start(f32[1,32,32]{2,1,0:T(8,128)S(1)} %get-tuple-element.393), channel_id=1, source_target_pairs={{4,0},{8,4},{12,8},{16,12},{20,16},{24,20},{28,24},{5,1},{9,5},{13... | collective-permute-start | bytes 12296 | tf_op jit(solution)/shard_map/ppermute | solution.py:15
  149.8 11.9 %collective-permute-start.2 = (f32[1,32,32]{2,1,0:T(8,128)S(1)}, f32[1,32,32]{2,1,0:T(8,128)S(1)}, u32[]{:S(2)}, u32[]{:S(2)}) collective-permute-start(f32[1,32,32]{2,1,0:T(8,128)S(1)} %get-tuple-element.384), channel_id=1, source_target_pairs={{0,4},{4,8},{8,12},{12,16},{16,20},{20,24},{24,28},{1,5},{5,9},{9,... | collective-permute-start | bytes 12296 | tf_op jit(solution)/shard_map/ppermute | solution.py:15
  154.8 99.2 %collective-permute-start.25 = (f32[1,32,512]{2,1,0:T(8,128)S(1)}, f32[1,32,512]{2,1,0:T(8,128)S(1)}, u32[]{:S(2)}, u32[]{:S(2)}) collective-permute-start(f32[1,32,512]{2,1,0:T(8,128)S(1)} %get-tuple-element.375), channel_id=1, source_target_pairs={{4,0},{8,4},{12,8},{16,12},{20,16},{24,20},{28,24},{5,1},{9,5},{13... | collective-permute-start | bytes 196616 | tf_op jit(solution)/shard_map/ppermute | solution.py:15
  156.3 98.0 %collective-permute-start.24 = (f32[1,32,512]{2,1,0:T(8,128)S(1)}, f32[1,32,512]{2,1,0:T(8,128)S(1)}, u32[]{:S(2)}, u32[]{:S(2)}) collective-permute-start(f32[1,32,512]{2,1,0:T(8,128)S(1)} %get-tuple-element.374), channel_id=1, source_target_pairs={{0,4},{4,8},{8,12},{12,16},{16,20},{20,24},{24,28},{1,5},{5,9},{9,... | collective-permute-start | bytes 196616 | tf_op jit(solution)/shard_map/ppermute | solution.py:15
  161.7 24.0 %collective-permute-start.14 = (f32[2,32,32]{2,1,0:T(8,128)S(1)}, f32[2,32,32]{2,1,0:T(8,128)S(1)}, u32[]{:S(2)}, u32[]{:S(2)}) collective-permute-start(f32[2,32,32]{2,1,0:T(8,128)S(1)} %fusion.108), channel_id=1, source_target_pairs={{4,0},{8,4},{12,8},{16,12},{20,16},{24,20},{28,24},{5,1},{9,5},{13... | collective-permute-start | bytes 24584 | tf_op jit(solution)/shard_map/ppermute | solution.py:15
  163.2 34.3 %collective-permute-start.9 = (f32[2,32,32]{2,1,0:T(8,128)S(1)}, f32[2,32,32]{2,1,0:T(8,128)S(1)}, u32[]{:S(2)}, u32[]{:S(2)}) collective-permute-start(f32[2,32,32]{2,1,0:T(8,128)S(1)} %fusion.108), channel_id=1, source_target_pairs={{0,4},{4,8},{8,12},{12,16},{16,20},{20,24},{24,28},{1,5},{5,9},{9,... | collective-permute-start | bytes 24584 | tf_op jit(solution)/shard_map/ppermute | solution.py:15
  180.7 27.7 %collective-permute-start.12 = (f32[2,32,32]{2,1,0:T(8,128)S(1)}, f32[2,32,32]{2,1,0:T(8,128)S(1)}, u32[]{:S(2)}, u32[]{:S(2)}) collective-permute-start(f32[2,32,32]{2,1,0:T(8,128)S(1)} %fusion.104), channel_id=1, source_target_pairs={{0,4},{4,8},{8,12},{12,16},{16,20},{20,24},{24,28},{1,5},{5,9},{9,... | collective-permute-start | bytes 24584 | tf_op jit(solution)/shard_map/ppermute | solution.py:15
  196.0 39.8 %collective-permute-start.20 = (f32[2,32,32]{2,1,0:T(8,128)S(1)}, f32[2,32,32]{2,1,0:T(8,128)S(1)}, u32[]{:S(2)}, u32[]{:S(2)}) collective-permute-start(f32[2,32,32]{2,1,0:T(8,128)S(1)} %fusion.202), channel_id=1, source_target_pairs={{8,0},{12,4},{16,8},{20,12},{24,16},{28,20},{9,1},{13,5},{17,9},{2... | collective-permute-start | bytes 24584 | tf_op jit(solution)/shard_map/ppermute | solution.py:15
  197.5 32.4 %collective-permute-start.15 = (f32[2,32,32]{2,1,0:T(8,128)S(1)}, f32[2,32,32]{2,1,0:T(8,128)S(1)}, u32[]{:S(2)}, u32[]{:S(2)}) collective-permute-start(f32[2,32,32]{2,1,0:T(8,128)S(1)} %fusion.202), channel_id=1, source_target_pairs={{0,8},{4,12},{8,16},{12,20},{16,24},{20,28},{1,9},{5,13},{9,17},{1... | collective-permute-start | bytes 24584 | tf_op jit(solution)/shard_map/ppermute | solution.py:15
  225.9 15.6 %collective-permute-start.18 = (f32[2,32,32]{2,1,0:T(8,128)S(1)}, f32[2,32,32]{2,1,0:T(8,128)S(1)}, u32[]{:S(2)}, u32[]{:S(2)}) collective-permute-start(f32[2,32,32]{2,1,0:T(8,128)S(1)} %fusion.192), channel_id=1, source_target_pairs={{0,8},{4,12},{8,16},{12,20},{16,24},{20,28},{1,9},{5,13},{9,17},{1... | collective-permute-start | bytes 24584 | tf_op jit(solution)/shard_map/ppermute | solution.py:15
  234.6 8.4 %collective-permute-start.22 = (f32[2,32,32]{2,1,0:T(8,128)S(1)}, f32[2,32,32]{2,1,0:T(8,128)S(1)}, u32[]{:S(2)}, u32[]{:S(2)}) collective-permute-start(f32[2,32,32]{2,1,0:T(8,128)S(1)} %fusion.213), channel_id=1, source_target_pairs={{16,0},{20,4},{24,8},{28,12},{17,1},{21,5},{25,9},{29,13},{18,2},{... | collective-permute-start | bytes 24584 | tf_op jit(solution)/shard_map/ppermute | solution.py:15
  235.9 8.8 %collective-permute-start.19 = (f32[2,32,32]{2,1,0:T(8,128)S(1)}, f32[2,32,32]{2,1,0:T(8,128)S(1)}, u32[]{:S(2)}, u32[]{:S(2)}) collective-permute-start(f32[2,32,32]{2,1,0:T(8,128)S(1)} %fusion.213), channel_id=1, source_target_pairs={{0,16},{4,20},{8,24},{12,28},{1,17},{5,21},{9,25},{13,29},{2,18},{... | collective-permute-start | bytes 24584 | tf_op jit(solution)/shard_map/ppermute | solution.py:15
  241.5 8.4 %collective-permute-start.21 = (f32[2,32,32]{2,1,0:T(8,128)S(1)}, f32[2,32,32]{2,1,0:T(8,128)S(1)}, u32[]{:S(2)}, u32[]{:S(2)}) collective-permute-start(f32[2,32,32]{2,1,0:T(8,128)S(1)} %fusion.214), channel_id=1, source_target_pairs={{0,16},{4,20},{8,24},{12,28},{1,17},{5,21},{9,25},{13,29},{2,18},{... | collective-permute-start | bytes 24584 | tf_op jit(solution)/shard_map/ppermute | solution.py:15
  263.3 8.0 %collective-permute-start.29 = (f32[2,32,512]{2,1,0:T(8,128)S(1)}, f32[2,32,512]{2,1,0:T(8,128)S(1)}, u32[]{:S(2)}, u32[]{:S(2)}) collective-permute-start(f32[2,32,512]{2,1,0:T(8,128)S(1)} %fusion.40), channel_id=1, source_target_pairs={{8,0},{12,4},{16,8},{20,12},{24,16},{28,20},{9,1},{13,5},{17,9},{2... | collective-permute-start | bytes 393224 | tf_op jit(solution)/shard_map/ppermute | solution.py:15
  264.8 8.2 %collective-permute-start.28 = (f32[2,32,512]{2,1,0:T(8,128)S(1)}, f32[2,32,512]{2,1,0:T(8,128)S(1)}, u32[]{:S(2)}, u32[]{:S(2)}) collective-permute-start(f32[2,32,512]{2,1,0:T(8,128)S(1)} %fusion.40), channel_id=1, source_target_pairs={{0,8},{4,12},{8,16},{12,20},{16,24},{20,28},{1,9},{5,13},{9,17},{1... | collective-permute-start | bytes 393224 | tf_op jit(solution)/shard_map/ppermute | solution.py:15
  273.3 8.1 %collective-permute-start.31 = (f32[2,32,512]{2,1,0:T(8,128)S(1)}, f32[2,32,512]{2,1,0:T(8,128)S(1)}, u32[]{:S(2)}, u32[]{:S(2)}) collective-permute-start(f32[2,32,512]{2,1,0:T(8,128)S(1)} %fusion.41), channel_id=1, source_target_pairs={{16,0},{20,4},{24,8},{28,12},{17,1},{21,5},{25,9},{29,13},{18,2},{... | collective-permute-start | bytes 393224 | tf_op jit(solution)/shard_map/ppermute | solution.py:15
  274.8 8.3 %collective-permute-start.30 = (f32[2,32,512]{2,1,0:T(8,128)S(1)}, f32[2,32,512]{2,1,0:T(8,128)S(1)}, u32[]{:S(2)}, u32[]{:S(2)}) collective-permute-start(f32[2,32,512]{2,1,0:T(8,128)S(1)} %fusion.41), channel_id=1, source_target_pairs={{0,16},{4,20},{8,24},{12,28},{1,17},{5,21},{9,25},{13,29},{2,18},{... | collective-permute-start | bytes 393224 | tf_op jit(solution)/shard_map/ppermute | solution.py:15
  290.3 48.0 %collective-permute-start.32 = (f32[16,32,1,128]{3,2,1,0:T(1,128)S(1)}, f32[16,32,1,128]{3,2,1,0:T(1,128)S(1)}, u32[]{:S(2)}, u32[]{:S(2)}) collective-permute-start(f32[16,32,1,128]{3,2,1,0:T(1,128)S(1)} %get-tuple-element.370), channel_id=1, source_target_pairs={{0,1},{1,2},{2,3},{4,5},{5,6},{6,7},{8,9},{9,10},{10,11},{12,13},{... | collective-permute-start | bytes 786440 | tf_op jit(solution)/shard_map/ppermute | solution.py:26
  291.6 46.7 %collective-permute-start.33 = (f32[16,32,1,128]{3,2,1,0:T(1,128)S(1)}, f32[16,32,1,128]{3,2,1,0:T(1,128)S(1)}, u32[]{:S(2)}, u32[]{:S(2)}) collective-permute-start(f32[16,32,1,128]{3,2,1,0:T(1,128)S(1)} %get-tuple-element.371), channel_id=1, source_target_pairs={{1,0},{2,1},{3,2},{5,4},{6,5},{7,6},{9,8},{10,9},{11,10},{13,12},{... | collective-permute-start | bytes 786440 | tf_op jit(solution)/shard_map/ppermute | solution.py:28
  (23 other events, 812.5 us)
where the time goes:
time: 349 us; the launch traced here: 345 us
  matrix products  112 us (32%)
  starting transfers between devices  97.1 us (28%)
  blocking collectives  44.5 us (13%)
  waiting for transfers between devices  38.9 us (11%)
  local copies, waits for them, and re-layouts  35.3 us (10%)
  other arithmetic  11.6 us (3%)
    dot_general x468, matrix products, product(): return jnp.matmul(left_mat, right_mat, precision=exact_precision)  108 us
    ppermute x30, starting transfers between devices, passed_along(): lax.ppermute(value, axis, [(source, source + steps) for source in range(f...  88.4 us
    unnamed x1, blocking collectives  44.5 us
    ppermute x30, waiting for transfers between devices, passed_along(): lax.ppermute(value, axis, [(source, source + steps) for source in range(f...  38.9 us
    gather x19, local copies, waits for them, and re-layouts, invert(): diag_values = jnp.diagonal(matrices, axis1=-2, axis2=-1)  13.5 us
    mul x14, local copies, waits for them, and re-layouts, backward(): field_next = product(inverse_now, field_now - c_vec[:, None] * field_next)  9.6 us
  transfers between devices with their start and end apart: 34, of which 14 were waited for; matrix products, arithmetic and copies ran while one was open for 42% of the time, Pallas kernels for 0%

commit v1 on v0

v1 whole, which is shorter than its diff:
```python
import functools

import jax
import jax.numpy as jnp
from jax import lax
from jax.experimental import pallas as pl
from jax.experimental.pallas import tpu as pltpu
from jax.sharding import PartitionSpec as P

SEG_DEV = 4
MESH = pl.DeviceIdType.MESH
exact = lax.Precision.HIGHEST


def dot(a, b):
    return jnp.dot(a, b, precision=exact, preferred_element_type=jnp.float32)


def invert(mats):
    size = mats[0].shape[0]
    row_id = lax.broadcasted_iota(jnp.int32, (size, size), 0)
    col_id = lax.broadcasted_iota(jnp.int32, (size, size), 1)
    for k in range(size):
        done = []
        for a in mats:
            pivot = 1.0 / a[k : k + 1, k : k + 1]
            row = jnp.where(col_id[:1] == k, 1.0, a[k : k + 1, :]) * pivot
            col = a[:, k : k + 1]
            rest = jnp.where(col_id == k, 0.0, a) - col * row
            done.append(jnp.where(row_id == k, row, rest))
        mats = done
    return mats


def kernel(n, nc, cot, diag, low, up, prof_rate, open_ref, out, emit, G, F, X, V, msg_out, msg_in, back_out, back_in,
           edge_out, edge_in, s_msg, r_msg, s_back, r_back, s_hal, r_hal, s_edge, r_edge):
    cells, nb = diag.shape[0], diag.shape[1]
    size = cells * nb
    rows = cot.shape[0] // size
    nz = cot.shape[1]
    per = rows * nz // n
    a = lax.axis_index("axial")
    c = lax.axis_index("cross")
    has_lo = c > 0
    has_hi = c < nc - 1

    barrier = pltpu.get_barrier_semaphore()
    for off in range(1, n):
        pl.semaphore_signal(barrier, inc=1, device_id=(lax.rem(a + off, n), c), device_id_type=MESH)

    @pl.when(has_lo)
    def _():
        pl.semaphore_signal(barrier, inc=1, device_id=(a, c - 1), device_id_type=MESH)

    @pl.when(has_hi)
    def _():
        pl.semaphore_signal(barrier, inc=1, device_id=(a, c + 1), device_id_type=MESH)

    for y in range(rows):
        F[:, (y + 1) * nz : (y + 2) * nz] = cot[pl.ds(y, size, stride=rows), :]

    pl.semaphore_wait(barrier, n - 1 + has_lo.astype(jnp.int32) + has_hi.astype(jnp.int32))

    def hal_copy(down):
        src = F.at[:, nz : 2 * nz] if down else F.at[:, rows * nz : (rows + 1) * nz]
        dst = F.at[:, (rows + 1) * nz : (rows + 2) * nz] if down else F.at[:, 0:nz]
        way = 0 if down else 1
        return pltpu.make_async_remote_copy(
            src_ref=src, dst_ref=dst, send_sem=s_hal.at[way], recv_sem=r_hal.at[way],
            device_id=(a, c - 1 if down else c + 1), device_id_type=MESH)

    def edge_copy(down):
        way = 0 if down else 1
        return pltpu.make_async_remote_copy(
            src_ref=edge_out.at[way], dst_ref=edge_in.at[way], send_sem=s_edge.at[way], recv_sem=r_edge.at[way],
            device_id=(a, c - 1 if down else c + 1), device_id_type=MESH)

    @pl.when(has_lo)
    def _():
        hal_copy(True).start()

    @pl.when(has_hi)
    def _():
        hal_copy(False).start()

    @pl.when(jnp.logical_not(has_lo))
    def _():
        F[:, 0:nz] = jnp.zeros((size, nz), jnp.float32)

    @pl.when(jnp.logical_not(has_hi))
    def _():
        F[:, (rows + 1) * nz : (rows + 2) * nz] = jnp.zeros((size, nz), jnp.float32)

    V[...] = jnp.zeros(V.shape, jnp.float32)
    V[0:cells, 0:nb] = low[...]
    V[cells : 2 * cells, 0:nb] = up[...]
    V[2 * cells : 2 * cells + 2, 0:nb] = prof_rate[...]
    V[...] = V[...].T
    low_col = [V[0:nb, j : j + 1] for j in range(cells)]
    up_col = [V[0:nb, cells + j : cells + j + 1] for j in range(cells)]
    cross_col = V[0:nb, 2 * cells : 2 * cells + 1]
    prof_col = V[0:nb, 2 * cells + 1 : 2 * cells + 2]

    eye = (lax.broadcasted_iota(jnp.int32, (nb, nb), 0) == lax.broadcasted_iota(jnp.int32, (nb, nb), 1)).astype(jnp.float32)

    G[...] = jnp.zeros(G.shape, jnp.float32)
    inverses = invert([diag[i] for i in range(cells)])
    pack = 128 // nb
    same = (lax.broadcasted_iota(jnp.int32, (128, 128), 0) // nb) == (lax.broadcasted_iota(jnp.int32, (128, 128), 1) // nb)
    for g in range(cells // pack):
        tall = jnp.concatenate(inverses[g * pack : (g + 1) * pack], axis=0)
        wide = jnp.where(same, jnp.concatenate([tall] * pack, axis=1), 0.0)
        G[g * 128 : (g + 1) * 128, g * 128 : (g + 1) * 128] = wide.T
    chunk = 1
    while chunk < cells:
        width = chunk * nb
        joints = list(range(chunk, cells, 2 * chunk))
        parts, weights = [], []
        for j in joints:
            o, m = (j - chunk) * nb, j * nb
            lp = up_col[j - 1] * G[m - nb : m, m - nb : m]
            rq = low_col[j] * G[m : m + nb, m : m + nb]
            weights.append(eye - dot(rq, lp))
            parts.append((o, m, lp, rq))
        weights = invert(weights)
        for j, (o, m, lp, rq), w in zip(joints, parts, weights):
            span = max(128, 2 * width)
            lo = o // span * span
            row_l = up_col[j - 1] * G[m - nb : m, lo : lo + span]
            row_r = low_col[j] * G[m : m + nb, lo : lo + span]
            p = dot(w, row_r + dot(rq, row_l))
            q = row_l + dot(lp, p)
            col_l = G[o:m, m - nb : m]
            col_r = G[m : m + width, m : m + nb]
            G[o:m, lo : lo + span] += dot(col_l, p)
            G[m : m + width, lo : lo + span] += dot(col_r, q)
        chunk *= 2

    head, tail = low_col[0], up_col[cells - 1]
    g_head, g_tail = G[0:nb, :], G[size - nb : size, :]
    ends = jnp.concatenate([head * g_head, tail * g_tail], axis=0)
    field = dot(ends, F[:, nz : (rows + 1) * nz])
    ports = jnp.concatenate([ends[:, 0:nb], ends[:, size - nb : size]], axis=1)
    for e in range(n):
        bits = [ports, field[:, e * per : (e + 1) * per]]
        if 2 * nb + per < 128:
            bits.append(jnp.zeros((2 * nb, 128 - 2 * nb - per), jnp.float32))
        msg_out[e] = jnp.concatenate(bits, axis=1)

    def msg_copy(off):
        peer = lax.rem(a + off, n)
        return pltpu.make_async_remote_copy(
            src_ref=msg_out.at[peer], dst_ref=msg_in.at[a], send_sem=s_msg.at[off], recv_sem=r_msg.at[off],
            device_id=(peer, c), device_id_type=MESH)

    def back_copy(off):
        peer = lax.rem(a + off, n)
        return pltpu.make_async_remote_copy(
            src_ref=back_out.at[peer], dst_ref=back_in.at[a], send_sem=s_back.at[off], recv_sem=r_back.at[off],
            device_id=(peer, c), device_id_type=MESH)

    for off in range(1, n):
        msg_copy(off).start()
    msg_in[a] = msg_out[a]

    half = rows * nz // 2
    for part in range(2):
        X[:, nz + part * half : nz + (part + 1) * half] = dot(G[...], F[:, nz + part * half : nz + (part + 1) * half])

    @pl.when(has_lo)
    def _():
        hal_copy(True).wait_send()
        hal_copy(False).wait_recv()

    @pl.when(has_hi)
    def _():
        hal_copy(False).wait_send()
        hal_copy(True).wait_recv()

    sides = dot(G[...], jnp.concatenate([F[:, 0:nz], F[:, (rows + 1) * nz : (rows + 2) * nz]], axis=1))
    X[:, 0:nz] = sides[:, 0:nz]
    X[:, (rows + 1) * nz : (rows + 2) * nz] = sides[:, nz : 2 * nz]

    for off in range(1, n):
        msg_copy(off).wait_recv()

    lane = lax.broadcasted_iota(jnp.int32, (1, 128), 1)
    keep_l = jnp.where((lane >= nb) & (lane < 2 * nb), 0.0, 1.0)
    keep_r = jnp.where(lane < nb, 0.0, 1.0)
    groups = [(msg_in[d][0:nb], msg_in[d][nb : 2 * nb], None) for d in range(n)]
    while len(groups) > 1:
        pairs = [(groups[i], groups[i + 1]) for i in range(0, len(groups), 2)]
        weights = invert([eye - dot(r[0][:, 0:nb], l[1][:, nb : 2 * nb]) for l, r in pairs])
        top = len(pairs) == 1
        groups = []
        for (l, r), w in zip(pairs, weights):
            from_l, from_r = l[1] * keep_l, r[0] * keep_r
            p = dot(w, from_r + dot(r[0][:, 0:nb], from_l))
            q = from_l + dot(l[1][:, nb : 2 * nb], p)
            left = l[0] if l[2] is None else jnp.concatenate([l[0], l[2]], axis=0)
            right = r[1] if r[2] is None else jnp.concatenate([r[1], r[2]], axis=0)
            left = left * keep_l + dot(left[:, nb : 2 * nb], p)
            right = right * keep_r + dot(right[:, 0:nb], q)
            inner = [p, q]
            if l[2] is not None:
                inner = [left[nb:]] + inner
            if r[2] is not None:
                inner = inner + [right[nb:]]
            groups.append((left[0:nb], right[0:nb], jnp.concatenate(inner, axis=0)))
    inner = groups[0][2]
    none = jnp.zeros((nb, 128), jnp.float32)
    for d in range(n):
        if d == 0:
            back_out[d] = jnp.concatenate([none, inner[0:nb]], axis=0)
        elif d == n - 1:
            back_out[d] = jnp.concatenate([inner[(2 * d - 1) * nb :], none], axis=0)
        else:
            back_out[d] = inner[(2 * d - 1) * nb : (2 * d + 1) * nb]
    for off in range(1, n):
        back_copy(off).start()
    back_in[a] = back_out[a]
    for off in range(1, n):
        back_copy(off).wait_recv()

    each = n // rows
    flux = []
    for y in range(rows):
        flux.append(jnp.concatenate([back_in[y * each + e][:, 2 * nb : 2 * nb + per] for e in range(each)], axis=1))
    edge_out[0] = flux[0]
    edge_out[1] = flux[rows - 1]

    @pl.when(has_lo)
    def _():
        edge_copy(True).start()

    @pl.when(has_hi)
    def _():
        edge_copy(False).start()

    gc = jnp.concatenate([G[:, 0:nb], G[:, size - nb : size]], axis=1)
    X[:, nz : (rows + 1) * nz] += dot(gc, jnp.concatenate(flux, axis=1))

    @pl.when(has_lo)
    def _():
        edge_copy(True).wait_send()
        edge_copy(False).wait_recv()
        X[:, 0:nz] += dot(gc, edge_in[1])

    @pl.when(has_hi)
    def _():
        edge_copy(False).wait_send()
        edge_copy(True).wait_recv()
        X[:, (rows + 1) * nz : (rows + 2) * nz] += dot(gc, edge_in[0])

    opens = []
    for y in range(-1, rows + 1):
        at = jnp.clip(c * rows + y, 0, nc * rows - 1)
        line = open_ref[pl.ds(at, 1), :].astype(jnp.float32)
        if y == -1:
            line = jnp.where(has_lo, line, 0.0)
        if y == rows:
            line = jnp.where(has_hi, line, 0.0)
        opens.append(line)
    zlane = lax.broadcasted_iota(jnp.int32, (1, nz), 1)
    step_col = jnp.concatenate([cross_col] * 4, axis=0)
    share_col = jnp.concatenate([prof_col] * 4, axis=0)
    block = 4 * nb
    for y in range(rows):
        here = opens[y + 1]
        before = jnp.where(zlane == 0, 0.0, pltpu.roll(here, 1, 1)) * here
        after = jnp.where(zlane == nz - 1, 0.0, pltpu.roll(here, nz - 1, 1)) * here
        above = opens[y] * here
        below = opens[y + 2] * here
        total = before + after + above + below
        for i in range(size // block):
            at = slice(i * block, (i + 1) * block)
            x = X[at, (y + 1) * nz : (y + 2) * nz]
            moved = (above * (X[at, y * nz : (y + 1) * nz] - x) + below * (X[at, (y + 2) * nz : (y + 3) * nz] - x)
                     + before * (pltpu.roll(x, 1, 1) - x) + after * (pltpu.roll(x, nz - 1, 1) - x))
            out[pl.ds(i * block * rows + y, block, stride=rows), :] = x + step_col * moved
            sent = x * here * share_col
            for k in range(4):
                emit[y, pl.ds(i * 4 + k, 1), :] = jnp.sum(sent[k * nb : (k + 1) * nb], axis=0, keepdims=True)

    for off in range(1, n):
        msg_copy(off).wait_send()
        back_copy(off).wait_send()


def per_device(n, nc, cotangent, diag_blocks, lower_rates, upper_rates, cross_rate, bin_profile, open_cells, segment_ids):
    cells, nb, rows, nz = cotangent.shape
    size = cells * nb
    vmem = pl.BlockSpec(memory_space=pltpu.VMEM)
    dma = pltpu.SemaphoreType.DMA
    grad, emit = pl.pallas_call(
        functools.partial(kernel, n, nc),
        out_shape=(
            jax.ShapeDtypeStruct((size * rows, nz), jnp.float32),
            jax.ShapeDtypeStruct((rows, cells, nz), jnp.float32),
        ),
        in_specs=[vmem] * 6,
        out_specs=(vmem, vmem),
        scratch_shapes=[
            pltpu.VMEM((size, size), jnp.float32),
            pltpu.VMEM((size, (rows + 2) * nz), jnp.float32),
            pltpu.VMEM((size, (rows + 2) * nz), jnp.float32),
            pltpu.VMEM((128, 128), jnp.float32),
            pltpu.VMEM((n, 2 * nb, 128), jnp.float32),
            pltpu.VMEM((n, 2 * nb, 128), jnp.float32),
            pltpu.VMEM((n, 2 * nb, 128), jnp.float32),
            pltpu.VMEM((n, 2 * nb, 128), jnp.float32),
            pltpu.VMEM((2, 2 * nb, nz), jnp.float32),
            pltpu.VMEM((2, 2 * nb, nz), jnp.float32),
            dma((n,)), dma((n,)), dma((n,)), dma((n,)), dma((2,)), dma((2,)), dma((2,)), dma((2,)),
        ],
        compiler_params=pltpu.CompilerParams(
            collective_id=0, has_side_effects=True, vmem_limit_bytes=48 * 1024 * 1024
        ),
    )(
        cotangent.reshape(size * rows, nz), diag_blocks, lower_rates, upper_rates,
        jnp.stack([cross_rate, bin_profile]), open_cells,
    )
    emitted = jnp.sum(emit, axis=-1).T / nz
    wanted = lax.iota(jnp.int32, SEG_DEV * n * nc)
    onehot = (segment_ids.reshape(-1)[:, None] == wanted[None, :]).astype(jnp.float32)
    grad_emission = lax.psum_scatter(
        jnp.dot(emitted.reshape(-1), onehot, precision=exact), ("axial", "cross"), scatter_dimension=0, tiled=True
    )
    return grad.reshape(cotangent.shape), grad_emission


def solution(mesh):
    in_specs = (
        P("axial", None, "cross", None),
        P("axial", None, None),
        P("axial", None),
        P("axial", None),
        P(),
        P(),
        P(),
        P("axial", "cross"),
    )
    out_specs = (P("axial", None, "cross", None), P(("axial", "cross")))
    return jax.shard_map(
        functools.partial(per_device, mesh.shape["axial"], mesh.shape["cross"]),
        mesh=mesh, in_specs=in_specs, out_specs=out_specs, check_vma=False,
    )
```

time: 349 us -> 112 us (0.32); the launches traced: 345 us -> 112 us
  matrix products: 112 us -> 0.19 us
  starting transfers between devices: 97.1 us -> 0 us
  Pallas kernels: 0 us -> 62.2 us
  waiting for transfers between devices: 38.9 us -> 0 us
  local copies, waits for them, and re-layouts: 35.3 us -> 7.41 us
  other arithmetic: 11.6 us -> 0.1 us
    dot_general x471 -> x1, matrix products: 112 us -> 0.19 us  [per_device(): jnp.dot(emitted.reshape(-1), onehot, precision=exact)]
    ppermute x34 -> x0, starting transfers between devices: 97.1 us -> none  [the longest x30 88.4 us: passed_along(): lax.ppermute(value, axis, [(source, source + steps) for source in range(f...]
    pallas_call x0 -> x1, Pallas kernels: none -> 62.2 us  [per_device(): pl.pallas_call(functools.partial(kernel, n, nc), out_shape=(jax.ShapeDtyp...]
    ppermute x34 -> x0, waiting for transfers between devices: 38.9 us -> none  [the longest x30 38.9 us: passed_along(): lax.ppermute(value, axis, [(source, source + steps) for source in range(f...]
    gather x19 -> x0, local copies, waits for them, and re-layouts: 13.5 us -> none  [invert(): diag_values = jnp.diagonal(matrices, axis1=-2, axis2=-1)]
    mul x28 -> x0, local copies, waits for them, and re-layouts: 9.78 us -> none  [the longest x14 9.6 us: backward(): field_next = product(inverse_now, field_now - c_vec[:, None] * field_next)]
    unnamed x29 -> x19, local copies, waits for them, and re-layouts: 2.5 us -> 7.14 us
    slice x9 -> x0, local copies, waits for them, and re-layouts: 4.38 us -> none  [the longest x2 1.61 us: per_device(): source_all[1:last_cell]]
  transfers between devices with their start and end apart: 34 -> 0, of which waited for: 14 -> 0; matrix products, arithmetic and copies ran while one was open for 42% -> 0% of each run, Pallas kernels for 0% -> 0%
where the time goes in v1:
time: 112 us
  Pallas kernels  62.2 us (56%)
  blocking collectives  41.5 us (37%)
  local copies, waits for them, and re-layouts  7.41 us (7%)
    pallas_call x1, Pallas kernels, per_device(): pl.pallas_call(functools.partial(kernel, n, nc), out_shape=(jax.ShapeDtyp...  62.2 us
    unnamed x1, blocking collectives  41.5 us
    unnamed x19, local copies, waits for them, and re-layouts  7.14 us

profile of v1, /device:TPU:0, one launch (start us, length us, event | category | flops | bytes accessed | tf_op | source)
XLA Modules:
  0.0 112.1 jit_solution(7448690096789913033)
XLA Ops:
  0.6 0.0 copy-start.6
  0.6 0.0 copy-start.7
  0.6 0.6 copy-done.6
  1.3 0.0 copy-done.7
  1.3 0.0 copy-start
  1.3 1.2 %copy-done = f32[16,32,4,128]{3,2,1,0:T(4,128)S(1)} copy-done((f32[16,32,4,128]{3,2,1,0:T(4,128)S(1)}, f32[16,32,4,128]{3,2,1,0:T(4,128)}, u32[]{:S(2)}) %copy-start) | copy-done | bytes 1048600
  2.5 0.0 copy-start.1
  2.5 0.9 copy-done.1
  3.5 0.0 copy-start.2
  3.5 0.7 copy-done.2
  4.2 0.0 copy-start.3
  4.2 0.7 copy-done.3
  4.9 0.7 copy-done.4
  5.6 62.2 %shard_map.95 = (f32[2048,128]{1,0:T(8,128)S(1)}, f32[4,16,128]{2,1,0:T(8,128)S(1)}) custom-call(f32[2048,128]{1,0:T(8,128)S(1)} %bitcast.9, f32[16,32,32]{2,1,0:T(8,128)S(1)} %copy-done.1, f32[16,32]{1,0:T(8,128)S(1)} %copy-done.2, f32[16,32]{1,0:T(8,128)S(1)} %copy-done.3, f32[2,32]{1,0:T(2,128)S(1)} %pad_maximum_fusion.prof_rate, s32[16,128]{1,0:T(8,128)S(1)} %copy-done.4), custom_call_target="tpu_custom_call" | custom-call | tf_op jit(solution)/shard_map/pallas_call | solution.py:295
  67.8 0.1 reduce_sum.9
  67.9 0.1 copy.12
  68.0 0.1 reshape.17
  68.0 0.6 copy-done.5
  68.6 0.1 copy.13
  68.7 0.1 eq.15
  68.8 0.2 convolution_bitcast_fusion
  69.0 41.5 %all-reduce = f32[128]{0:T(128)S(1)} all-reduce(f32[128]{0:T(128)S(1)} %convolution_bitcast_fusion), channel_id=2, replica_groups=mesh['axial'=8,'cross'=4] {'axial','cross'}, use_global_device_ids=true, to_apply=%region_1.0.clone | all-reduce | flops 128 | bytes 1024
  110.5 0.6 dynamic-slice
  111.1 1.0 copy.15
  (4 shorter events, 0.0 us)
Async XLA Ops:
  0.6 0.7 copy-start.6
  0.6 0.7 copy-start.7
  1.3 1.2 %copy-start = (f32[16,32,4,128]{3,2,1,0:T(4,128)S(1)}, f32[16,32,4,128]{3,2,1,0:T(4,128)}, u32[]{:S(2)}) copy-start(f32[16,32,4,128]{3,2,1,0:T(4,128)} %param.8) | copy-start | bytes 3145732
  2.5 0.9 copy-start.1
  3.5 0.7 copy-start.2
  4.2 0.7 copy-start.3
  4.9 0.7 copy-start.4
  68.0 0.7 copy-start.5

commit v2 on v1

--- a/solution.py
+++ b/solution.py
@@ -32,8 +32,15 @@
     return mats
 
 
-def kernel(n, nc, cot, diag, low, up, prof_rate, open_ref, out, emit, G, F, X, V, msg_out, msg_in, back_out, back_in,
-           edge_out, edge_in, s_msg, r_msg, s_back, r_back, s_hal, r_hal, s_edge, r_edge):
+def kernel(n, nc, cot_hbm, diag_hbm, low_hbm, up_hbm, cross_hbm, prof_hbm, open_hbm, seg_hbm, out, out_seg,
+           cot, diag, low, up, cross_rate, prof_rate, open_ref, seg, G, F, X, V, msg_out, msg_in, back_out, back_in,
+           edge_out, edge_in, sum_out, sum_cross, sum_axial, s_in, s_msg, r_msg, s_back, r_back, s_hal, r_hal,
+           s_edge, r_edge, s_cross, r_cross, s_axial, r_axial):
+    pairs_in = [(cot_hbm, cot), (diag_hbm, diag), (low_hbm, low), (up_hbm, up), (cross_hbm, cross_rate), (prof_hbm, prof_rate),
+                (open_hbm, open_ref), (seg_hbm, seg)]
+    loads = [pltpu.make_async_copy(src, dst, s_in.at[i]) for i, (src, dst) in enumerate(pairs_in)]
+    for i in (1, 0, 2, 3, 4, 5, 6, 7):
+        loads[i].start()
     cells, nb = diag.shape[0], diag.shape[1]
     size = cells * nb
     rows = cot.shape[0] // size
@@ -48,18 +55,17 @@
     for off in range(1, n):
         pl.semaphore_signal(barrier, inc=1, device_id=(lax.rem(a + off, n), c), device_id_type=MESH)
 
-    @pl.when(has_lo)
-    def _():
-        pl.semaphore_signal(barrier, inc=1, device_id=(a, c - 1), device_id_type=MESH)
-
-    @pl.when(has_hi)
-    def _():
-        pl.semaphore_signal(barrier, inc=1, device_id=(a, c + 1), device_id_type=MESH)
-
+    for off in range(1, nc):
+        pl.semaphore_signal(barrier, inc=1, device_id=(a, lax.rem(c + off, nc)), device_id_type=MESH)
+
+    loads[1].wait()
+    inverses = invert([diag[i] for i in range(cells)])
+
+    loads[0].wait()
     for y in range(rows):
         F[:, (y + 1) * nz : (y + 2) * nz] = cot[pl.ds(y, size, stride=rows), :]
 
-    pl.semaphore_wait(barrier, n - 1 + has_lo.astype(jnp.int32) + has_hi.astype(jnp.int32))
+    pl.semaphore_wait(barrier, n - 1 + nc - 1)
 
     def hal_copy(down):
         src = F.at[:, nz : 2 * nz] if down else F.at[:, rows * nz : (rows + 1) * nz]
@@ -91,20 +97,24 @@
     def _():
         F[:, (rows + 1) * nz : (rows + 2) * nz] = jnp.zeros((size, nz), jnp.float32)
 
+    for i in range(2, 8):
+        loads[i].wait()
     V[...] = jnp.zeros(V.shape, jnp.float32)
     V[0:cells, 0:nb] = low[...]
     V[cells : 2 * cells, 0:nb] = up[...]
-    V[2 * cells : 2 * cells + 2, 0:nb] = prof_rate[...]
+    V[2 * cells : 2 * cells + 1, 0:nb] = cross_rate[...]
+    V[2 * cells + 1 : 2 * cells + 2, 0:nb] = prof_rate[...]
+    V[2 * cells + 2 : 2 * cells + 2 + rows, 0:cells] = seg[...].astype(jnp.float32)
     V[...] = V[...].T
     low_col = [V[0:nb, j : j + 1] for j in range(cells)]
     up_col = [V[0:nb, cells + j : cells + j + 1] for j in range(cells)]
     cross_col = V[0:nb, 2 * cells : 2 * cells + 1]
     prof_col = V[0:nb, 2 * cells + 1 : 2 * cells + 2]
+    seg_col = [V[0:cells, 2 * cells + 2 + y : 2 * cells + 3 + y] for y in range(rows)]
 
     eye = (lax.broadcasted_iota(jnp.int32, (nb, nb), 0) == lax.broadcasted_iota(jnp.int32, (nb, nb), 1)).astype(jnp.float32)
 
     G[...] = jnp.zeros(G.shape, jnp.float32)
-    inverses = invert([diag[i] for i in range(cells)])
     pack = 128 // nb
     same = (lax.broadcasted_iota(jnp.int32, (128, 128), 0) // nb) == (lax.broadcasted_iota(jnp.int32, (128, 128), 1) // nb)
     for g in range(cells // pack):
@@ -240,18 +250,6 @@
     gc = jnp.concatenate([G[:, 0:nb], G[:, size - nb : size]], axis=1)
     X[:, nz : (rows + 1) * nz] += dot(gc, jnp.concatenate(flux, axis=1))
 
-    @pl.when(has_lo)
-    def _():
-        edge_copy(True).wait_send()
-        edge_copy(False).wait_recv()
-        X[:, 0:nz] += dot(gc, edge_in[1])
-
-    @pl.when(has_hi)
-    def _():
-        edge_copy(False).wait_send()
-        edge_copy(True).wait_recv()
-        X[:, (rows + 1) * nz : (rows + 2) * nz] += dot(gc, edge_in[0])
-
     opens = []
     for y in range(-1, rows + 1):
         at = jnp.clip(c * rows + y, 0, nc * rows - 1)
@@ -261,9 +259,48 @@
         if y == rows:
             line = jnp.where(has_hi, line, 0.0)
         opens.append(line)
+
+    segs = sum_out.shape[-1]
+    seg_id = lax.broadcasted_iota(jnp.int32, (1, segs), 1)
+    gain = jnp.zeros((8, segs), jnp.float32)
+    for y in range(rows):
+        bits = []
+        for i in range(cells):
+            sent = X[i * nb : (i + 1) * nb, (y + 1) * nz : (y + 2) * nz] * prof_col
+            bits.append(jnp.sum(sent, axis=0, keepdims=True))
+        given = jnp.sum(jnp.concatenate(bits, axis=0) * opens[y + 1], axis=1, keepdims=True) * (1.0 / nz)
+        picked = jnp.where(seg_col[y] == seg_id.astype(jnp.float32), given, 0.0)
+        for i in range(cells // 8):
+            gain = gain + picked[i * 8 : (i + 1) * 8]
+    sum_out[0] = gain
+
+    def cross_copy(off):
+        return pltpu.make_async_remote_copy(
+            src_ref=sum_out.at[0], dst_ref=sum_cross.at[off], send_sem=s_cross.at[off], recv_sem=r_cross.at[off],
+            device_id=(a, lax.rem(c + off, nc)), device_id_type=MESH)
+
+    def axial_copy(off):
+        return pltpu.make_async_remote_copy(
+            src_ref=sum_out.at[1], dst_ref=sum_axial.at[off], send_sem=s_axial.at[off], recv_sem=r_axial.at[off],
+            device_id=(lax.rem(a + off, n), c), device_id_type=MESH)
+
+    for off in range(1, nc):
+        cross_copy(off).start()
+
+    @pl.when(has_lo)
+    def _():
+        edge_copy(True).wait_send()
+        edge_copy(False).wait_recv()
+        X[:, 0:nz] += dot(gc, edge_in[1])
+
+    @pl.when(has_hi)
+    def _():
+        edge_copy(False).wait_send()
+        edge_copy(True).wait_recv()
+        X[:, (rows + 1) * nz : (rows + 2) * nz] += dot(gc, edge_in[0])
+
     zlane = lax.broadcasted_iota(jnp.int32, (1, nz), 1)
     step_col = jnp.concatenate([cross_col] * 4, axis=0)
-    share_col = jnp.concatenate([prof_col] * 4, axis=0)
     block = 4 * nb
     for y in range(rows):
         here = opens[y + 1]
@@ -278,9 +315,32 @@
             moved = (above * (X[at, y * nz : (y + 1) * nz] - x) + below * (X[at, (y + 2) * nz : (y + 3) * nz] - x)
                      + before * (pltpu.roll(x, 1, 1) - x) + after * (pltpu.roll(x, nz - 1, 1) - x))
             out[pl.ds(i * block * rows + y, block, stride=rows), :] = x + step_col * moved
-            sent = x * here * share_col
-            for k in range(4):
-                emit[y, pl.ds(i * 4 + k, 1), :] = jnp.sum(sent[k * nb : (k + 1) * nb], axis=0, keepdims=True)
+        if y == 0:
+            gain = sum_out[0]
+            for off in range(1, nc):
+                cross_copy(off).wait_recv()
+                gain = gain + sum_cross[off]
+            sum_out[1] = gain
+            for off in range(1, n):
+                axial_copy(off).start()
+
+    gain = sum_out[1]
+    for off in range(1, n):
+        axial_copy(off).wait_recv()
+        gain = gain + sum_axial[off]
+    gain = jnp.sum(gain, axis=0, keepdims=True)
+    own = out_seg.shape[1]
+    own_id = lax.broadcasted_iota(jnp.int32, (1, own), 1)
+    result = jnp.zeros((1, own), jnp.float32)
+    for j in range(own):
+        mine = jnp.sum(jnp.where(seg_id == (a * nc + c) * own + j, gain, 0.0), axis=1, keepdims=True)
+        result = jnp.where(own_id == j, mine, result)
+    out_seg[...] = result
+
+    for off in range(1, nc):
+        cross_copy(off).wait_send()
+    for off in range(1, n):
+        axial_copy(off).wait_send()
 
     for off in range(1, n):
         msg_copy(off).wait_send()
@@ -290,43 +350,42 @@
 def per_device(n, nc, cotangent, diag_blocks, lower_rates, upper_rates, cross_rate, bin_profile, open_cells, segment_ids):
     cells, nb, rows, nz = cotangent.shape
     size = cells * nb
+    segs = SEG_DEV * n * nc
     vmem = pl.BlockSpec(memory_space=pltpu.VMEM)
+    hbm = pl.BlockSpec(memory_space=pltpu.HBM)
     dma = pltpu.SemaphoreType.DMA
-    grad, emit = pl.pallas_call(
+    f32 = jnp.float32
+    operands = (
+        cotangent.reshape(size * rows, nz), diag_blocks, lower_rates, upper_rates,
+        cross_rate.reshape(1, nb), bin_profile.reshape(1, nb), open_cells, segment_ids.T,
+    )
+    grad, gain = pl.pallas_call(
         functools.partial(kernel, n, nc),
-        out_shape=(
-            jax.ShapeDtypeStruct((size * rows, nz), jnp.float32),
-            jax.ShapeDtypeStruct((rows, cells, nz), jnp.float32),
-        ),
-        in_specs=[vmem] * 6,
+        out_shape=(jax.ShapeDtypeStruct((size * rows, nz), f32), jax.ShapeDtypeStruct((1, SEG_DEV), f32)),
+        in_specs=[hbm] * len(operands),
         out_specs=(vmem, vmem),
-        scratch_shapes=[
-            pltpu.VMEM((size, size), jnp.float32),
-            pltpu.VMEM((size, (rows + 2) * nz), jnp.float32),
-            pltpu.VMEM((size, (rows + 2) * nz), jnp.float32),
-            pltpu.VMEM((128, 128), jnp.float32),
-            pltpu.VMEM((n, 2 * nb, 128), jnp.float32),
-            pltpu.VMEM((n, 2 * nb, 128), jnp.float32),
-            pltpu.VMEM((n, 2 * nb, 128), jnp.float32),
-            pltpu.VMEM((n, 2 * nb, 128), jnp.float32),
-            pltpu.VMEM((2, 2 * nb, nz), jnp.float32),
-            pltpu.VMEM((2, 2 * nb, nz), jnp.float32),
-            dma((n,)), dma((n,)), dma((n,)), dma((n,)), dma((2,)), dma((2,)), dma((2,)), dma((2,)),
+        scratch_shapes=[pltpu.VMEM(x.shape, x.dtype) for x in operands] + [
+            pltpu.VMEM((size, size), f32),
+            pltpu.VMEM((size, (rows + 2) * nz), f32),
+            pltpu.VMEM((size, (rows + 2) * nz), f32),
+            pltpu.VMEM((128, 128), f32),
+            pltpu.VMEM((n, 2 * nb, 128), f32),
+            pltpu.VMEM((n, 2 * nb, 128), f32),
+            pltpu.VMEM((n, 2 * nb, 128), f32),
+            pltpu.VMEM((n, 2 * nb, 128), f32),
+            pltpu.VMEM((2, 2 * nb, nz), f32),
+            pltpu.VMEM((2, 2 * nb, nz), f32),
+            pltpu.VMEM((2, 8, segs), f32),
+            pltpu.VMEM((nc, 8, segs), f32),
+            pltpu.VMEM((n, 8, segs), f32),
+            dma((len(operands),)), dma((n,)), dma((n,)), dma((n,)), dma((n,)), dma((2,)), dma((2,)), dma((2,)), dma((2,)),
+            dma((nc,)), dma((nc,)), dma((n,)), dma((n,)),
         ],
         compiler_params=pltpu.CompilerParams(
-            collective_id=0, has_side_effects=True, vmem_limit_bytes=48 * 1024 * 1024
+            collective_id=0, has_side_effects=True, vmem_limit_bytes=63 * 1024 * 1024 + 512 * 1024
         ),
-    )(
-        cotangent.reshape(size * rows, nz), diag_blocks, lower_rates, upper_rates,
-        jnp.stack([cross_rate, bin_profile]), open_cells,
-    )
-    emitted = jnp.sum(emit, axis=-1).T / nz
-    wanted = lax.iota(jnp.int32, SEG_DEV * n * nc)
-    onehot = (segment_ids.reshape(-1)[:, None] == wanted[None, :]).astype(jnp.float32)
-    grad_emission = lax.psum_scatter(
-        jnp.dot(emitted.reshape(-1), onehot, precision=exact), ("axial", "cross"), scatter_dimension=0, tiled=True
-    )
-    return grad.reshape(cotangent.shape), grad_emission
+    )(*operands)
+    return grad.reshape(cotangent.shape), gain.reshape(SEG_DEV)
 
 
 def solution(mesh):

time: 112 us -> 71.3 us (0.64)
  blocking collectives: 41.5 us -> 0 us
  Pallas kernels: 62.2 us -> 67.7 us
  local copies, waits for them, and re-layouts: 7.41 us -> 2.81 us
    unnamed x1 -> x0, blocking collectives: 41.5 us -> none
    pallas_call x1, Pallas kernels: 62.2 us -> 67.7 us  [per_device(): pl.pallas_call(functools.partial(kernel, n, nc), out_shape=(jax.ShapeDtyp...]
    unnamed x19 -> x4, local copies, waits for them, and re-layouts: 7.14 us -> 2.81 us
where the time goes in v2:
time: 71.3 us; the launch traced here: 71.1 us
  Pallas kernels  67.7 us (95%)
  local copies, waits for them, and re-layouts  2.81 us (4%)
    pallas_call x1, Pallas kernels, per_device(): pl.pallas_call(functools.partial(kernel, n, nc), out_shape=(jax.ShapeDtyp...  67.7 us
    unnamed x4, local copies, waits for them, and re-layouts  2.81 us

profile of v2, /device:TPU:0, one launch (start us, length us, event | category | flops | bytes accessed | tf_op | source)
XLA Modules:
  0.0 71.1 jit_solution(5951640768856207244)
XLA Ops:
  0.6 67.7 %shard_map.95 = (f32[2048,128]{1,0:T(8,128)}, f32[1,4]{1,0:T(1,128)}) custom-call(f32[2048,128]{1,0:T(8,128)} %bitcast.6, f32[16,32,32]{2,1,0:T(8,128)} %diag_hbm.1, f32[16,32]{1,0:T(8,128)} %low_hbm.1, f32[16,32]{1,0:T(8,128)} %up_hbm.1, f32[1,32]{1,0:T(1,128)} %bitcast.9, f32[1,32]{1,0:T(1,128)} %bitcast.10, s32[16,128]{1,0:T(8,128)} %open_hbm.1, ...), custom_call_target="tpu_custom_call" | custom-call | tf_op jit(solution)/shard_map/pallas_call | solution.py:362
  68.3 0.0 copy-start
  68.3 2.3 %copy.12 = f32[16,32,4,128]{3,2,1,0:T(4,128)} copy(f32[16,32,4,128]{3,2,1,0:T(4,128)} %bitcast.7) | data formatting | bytes 2097152
  70.6 0.0 copy-done
  70.6 0.5 copy.13
Async XLA Ops:
  68.3 2.3 %copy-start = (f32[1,4]{1,0:T(1,128)S(1)}, f32[1,4]{1,0:T(1,128)}, u32[]{:S(2)}) copy-start(f32[1,4]{1,0:T(1,128)} %get-tuple-element.5) | copy-start | bytes 52

commit v3 on v2

--- a/solution.py
+++ b/solution.py
@@ -8,6 +8,8 @@
 from jax.sharding import PartitionSpec as P
 
 SEG_DEV = 4
+PANEL_FEW = 8
+PANEL_MANY = 4
 MESH = pl.DeviceIdType.MESH
 exact = lax.Precision.HIGHEST
 
@@ -18,18 +20,33 @@
 
 def invert(mats):
     size = mats[0].shape[0]
-    row_id = lax.broadcasted_iota(jnp.int32, (size, size), 0)
-    col_id = lax.broadcasted_iota(jnp.int32, (size, size), 1)
-    for k in range(size):
-        done = []
-        for a in mats:
-            pivot = 1.0 / a[k : k + 1, k : k + 1]
-            row = jnp.where(col_id[:1] == k, 1.0, a[k : k + 1, :]) * pivot
-            col = a[:, k : k + 1]
-            rest = jnp.where(col_id == k, 0.0, a) - col * row
-            done.append(jnp.where(row_id == k, row, rest))
-        mats = done
-    return mats
+    panel = PANEL_FEW if len(mats) <= 4 else PANEL_MANY
+    slabs = range(size // 8)
+    row_id = lax.broadcasted_iota(jnp.int32, (8, size), 0)
+    col_id = lax.broadcasted_iota(jnp.int32, (8, size), 1)
+    mats = [[a[s * 8 : (s + 1) * 8] for s in slabs] for a in mats]
+    for first in range(0, size, panel):
+        spread = [
+            [[jnp.broadcast_to(a[s][:, first + j : first + j + 1], (8, size)) for s in slabs] for j in range(panel)]
+            for a in mats
+        ]
+        for j in range(panel):
+            k = first + j
+            home, at = k // 8, k % 8
+            for i, a in enumerate(mats):
+                col = spread[i][j]
+                pivot = 1.0 / col[home][at : at + 1]
+                row = jnp.where(col_id[:1] == k, 1.0, a[home][at : at + 1]) * pivot
+                done = [jnp.where(col_id == k, 0.0, a[s]) - col[s] * row for s in slabs]
+                done[home] = jnp.where(row_id == at, row, done[home])
+                mats[i] = done
+                for m in range(j + 1, panel):
+                    other = spread[i][m]
+                    entry = other[home][at : at + 1] * pivot
+                    later = [other[s] - col[s] * entry for s in slabs]
+                    later[home] = jnp.where(row_id == at, entry, later[home])
+                    spread[i][m] = later
+    return [jnp.concatenate(a, axis=0) for a in mats]
 
 
 def kernel(n, nc, cot_hbm, diag_hbm, low_hbm, up_hbm, cross_hbm, prof_hbm, open_hbm, seg_hbm, out, out_seg,

time: 71.3 us -> 56.5 us (0.79)
  Pallas kernels: 67.7 us -> 52.9 us
    pallas_call x1, Pallas kernels: 67.7 us -> 52.9 us  [per_device(): pl.pallas_call(functools.partial(kernel, n, nc), out_shape=(jax.ShapeDtyp...]
where the time goes in v3:
time: 56.5 us; the launch traced here: 56.4 us
  Pallas kernels  52.9 us (94%)
  local copies, waits for them, and re-layouts  2.81 us (5%)
  between operations  0.65 us (1%)
    pallas_call x1, Pallas kernels, per_device(): pl.pallas_call(functools.partial(kernel, n, nc), out_shape=(jax.ShapeDtyp...  52.9 us
    unnamed x4, local copies, waits for them, and re-layouts  2.81 us

profile of v3, /device:TPU:0, one launch (start us, length us, event | category | flops | bytes accessed | tf_op | source)
XLA Modules:
  0.0 56.4 jit_solution(1564064401021438790)
XLA Ops:
  0.6 52.9 %shard_map.95 = (f32[2048,128]{1,0:T(8,128)}, f32[1,4]{1,0:T(1,128)}) custom-call(f32[2048,128]{1,0:T(8,128)} %bitcast.6, f32[16,32,32]{2,1,0:T(8,128)} %diag_hbm.1, f32[16,32]{1,0:T(8,128)} %low_hbm.1, f32[16,32]{1,0:T(8,128)} %up_hbm.1, f32[1,32]{1,0:T(1,128)} %bitcast.9, f32[1,32]{1,0:T(1,128)} %bitcast.10, s32[16,128]{1,0:T(8,128)} %open_hbm.1, ...), custom_call_target="tpu_custom_call" | custom-call | tf_op jit(solution)/shard_map/pallas_call | solution.py:379
  53.5 0.0 copy-start
  53.5 2.3 %copy.12 = f32[16,32,4,128]{3,2,1,0:T(4,128)} copy(f32[16,32,4,128]{3,2,1,0:T(4,128)} %bitcast.7) | data formatting | bytes 2097152
  55.8 0.0 copy-done
  55.8 0.5 copy.13
Async XLA Ops:
  53.5 2.3 %copy-start = (f32[1,4]{1,0:T(1,128)S(1)}, f32[1,4]{1,0:T(1,128)}, u32[]{:S(2)}) copy-start(f32[1,4]{1,0:T(1,128)} %get-tuple-element.5) | copy-start | bytes 52
